TPU v7x, 32 devices: a whole 2x2x4 slice. The times are simulated.
32 devices in a mesh: groups: 2 (over x), rows: 8 (over z, y), chan: 2 (over core).
Axes of the slice: x: 2, y: 2, z: 4, core: 2. Of those that a mesh axis runs over, the one named last changes fastest.
Arguments:
- pair: bfloat16 [768, 384, 128], P(('groups', 'rows')), parts along dimension 0, may hold values from -6 to 6
- seq_len: int32 [2], P('groups'), parts along dimension 0, may hold values from 192 to 384
- pair_mask: int32 [768, 384], P(('groups', 'rows')), parts along dimension 0, may hold values 0 or 1
- ln_in_gain: bfloat16 [2, 128], replicated, may hold values from 0.25 to 1.75
- w_proj: bfloat16 [2, 4, 128, 64], P(None, None, None, 'chan'), may hold values from -0.5 to 0.5
- w_gate: bfloat16 [2, 128, 128], replicated, may hold values from -0.5 to 0.5
- ln_out_gain: bfloat16 [2, 64], P(None, 'chan'), may hold values from 0.25 to 1.75
- w_out: bfloat16 [2, 64, 128], P(None, 'chan'), may hold values from -0.75 to 0.75
Outputs:
- pair_out: bfloat16 [768, 384, 128], P(('groups', 'rows', 'chan')), parts along dimension 0
There are 2 independent parts, one for each index of `groups`. A program takes and returns all parts, laid end to end along the dimension named above; an argument that names none is the same for every part. Nothing has to cross between parts.
Inputs may be any that keep to these rules, and one draw needn't show every extreme that they name: Tokens at and after seq_len are padding.
All inputs are finite; a program needn't handle non-finite values. No bound on the sum of `pair_mask` on one device may be relied on, other than what follows from the above.
Results may differ from a plain program's by a relative error of at most 0.008.
Values may be sent and summed in bfloat16 or wider, within the bound.
A program may use at most 128 MiB of HBM per device.

v0:
```python
import jax
import jax.numpy as jnp
from jax import lax
from jax.sharding import PartitionSpec as P


def normalize(values, gain_row, along_axis):
    average = jnp.mean(values, axis=along_axis, keepdims=True)
    squares_mean = jnp.mean(values * values, axis=along_axis, keepdims=True)
    spread = jnp.maximum(squares_mean - average * average, 0.0)
    return (values - average) * lax.rsqrt(spread + 1e-05) * gain_row


def outgoing(left_side, right_side):
    return jnp.einsum(
        "cik,cjk->cij",
        left_side,
        lax.all_gather(right_side, "rows", axis=1, tiled=True),
        preferred_element_type=jnp.float32,
    )


def incoming(left_side, right_side):
    columns_left = lax.all_to_all(left_side, "rows", split_axis=2, concat_axis=1, tiled=True)
    return jnp.einsum(
        "cki,ckj->cij",
        columns_left,
        lax.all_gather(right_side, "rows", axis=1, tiled=True),
        preferred_element_type=jnp.float32,
    )


def shards(pair, seq_len, pair_mask, ln_in_gain, w_proj, w_gate, ln_out_gain, w_out):
    rows_here = pair.shape[0]
    columns = pair.shape[1]
    features = pair.shape[2]
    half_rows = rows_here // 2
    channels_own = w_proj.shape[3]
    channel_total = channels_own * lax.axis_size("chan")
    row_start = lax.axis_index("rows") * rows_here
    core_start = lax.axis_index("chan") * half_rows
    valid_cols = (jnp.arange(columns) < seq_len[0]).astype(jnp.float32)
    valid_rows = lax.dynamic_slice_in_dim(valid_cols, row_start, rows_here)
    pair_weight = pair_mask.astype(jnp.float32) * valid_rows[:, None] * valid_cols[None, :]
    current = pair
    for layer_index in range(2):
        if layer_index == 1:
            current = lax.all_gather(current, "chan", axis=0, tiled=True)
        normed = normalize(
            current.astype(jnp.float32), ln_in_gain[layer_index].astype(jnp.float32), 2
        ).astype(jnp.bfloat16)
        flattened = normed.reshape(rows_here * columns, features)
        stacked = jnp.concatenate([w_proj[layer_index, which] for which in range(4)], axis=1)
        projected = jnp.dot(flattened, stacked, preferred_element_type=jnp.float32).T.reshape(
            4, channels_own, rows_here, columns
        )
        left_side = (pair_weight * jax.nn.sigmoid(projected[0]) * projected[1]).astype(jnp.bfloat16)
        right_side = (pair_weight * jax.nn.sigmoid(projected[2]) * projected[3]).astype(
            jnp.bfloat16
        )
        if layer_index == 0:
            product = outgoing(left_side, right_side)
        else:
            product = incoming(left_side, right_side)
        product = product.astype(jnp.bfloat16)
        normed_half = lax.dynamic_slice_in_dim(normed, core_start, half_rows, 0)
        current_half = lax.dynamic_slice_in_dim(current, core_start, half_rows, 0)
        gate_values = jax.nn.sigmoid(
            jnp.dot(
                normed_half.reshape(half_rows * columns, features),
                w_gate[layer_index],
                preferred_element_type=jnp.float32,
            )
        ).reshape(half_rows, columns, features)
        values = product.astype(jnp.float32)
        channel_sums, channel_squares = lax.psum(
            (jnp.sum(values, axis=0), jnp.sum(values * values, axis=0)), "chan"
        )
        average = channel_sums / channel_total
        spread = jnp.maximum(channel_squares / channel_total - average * average, 0.0)
        gain_col = ln_out_gain[layer_index].astype(jnp.float32)[:, None, None]
        scaled = ((values - average) * lax.rsqrt(spread + 1e-05) * gain_col).astype(jnp.bfloat16)
        out_weight = w_out[layer_index]
        update = lax.psum_scatter(
            jnp.einsum("cij,cd->ijd", scaled, out_weight, preferred_element_type=jnp.float32),
            "chan",
            scatter_dimension=0,
            tiled=True,
        )
        current = (current_half.astype(jnp.float32) + gate_values * update).astype(jnp.bfloat16)
    return current


def solution(mesh):
    in_specs = (
        P(("groups", "rows"), None, None),
        P("groups"),
        P(("groups", "rows"), None),
        P(),
        P(None, None, None, "chan"),
        P(),
        P(None, "chan"),
        P(None, "chan", None),
    )
    out_specs = P(("groups", "rows", "chan"), None, None)
    return jax.shard_map(shards, mesh=mesh, in_specs=in_specs, out_specs=out_specs, check_vma=False)
```

profile of v0, /device:TPU:0, one launch (start us, length us, event | category | flops | bytes accessed | tf_op | source)
XLA Modules:
  0.0 498.2 jit_solution(18087518534557781297)
XLA Ops:
  9.9 6.3 %convert_reduce_fusion.1 = (f32[48,384]{1,0:T(8,128)S(1)}, f32[48,384]{1,0:T(8,128)S(1)}) fusion(bf16[48,384,128]{2,1,0:T(8,128)(2,1)} %param.8), kind=kLoop, calls=%fused_computation.5 | loop fusion | flops 9400320 | bytes 4866048 | tf_op jit(solution)/shard_map/reduce_sum | solution.py:8
  16.2 6.0 %fusion.8 = bf16[48,384,128]{2,1,0:T(8,128)(2,1)S(1)} fusion(bf16[48,384,128]{2,1,0:T(8,128)(2,1)S(1)} %copy-done.2, f32[128]{0:T(128)S(1)} %get-tuple-element.48, f32[48,384]{1,0:T(8,128)S(1)} %get-tuple-element.36, f32[48,384]{1,0:T(8,128)S(1)} %get-tuple-element.35), kind=kLoop, calls=%fused_computation.16 | loop fusion | flops 11796480 | bytes 9585152 | tf_op jit(solution)/shard_map/convert_element_type | solution.py:51
  35.1 4.9 fusion.24
  40.0 140.7 %all-gather.4.cloned.1.call-done = bf16[32,384,384]{2,1,0:T(8,128)(2,1)} async-done(((bf16[32,48,384]{2,1,0:T(8,128)(2,1)}), bf16[32,384,384]{2,1,0:T(8,128)(2,1)}) %all-gather.4.cloned.1.call-update) | async-done | bytes 9437200 | tf_op jit(solution)/shard_map/all_gather | solution.py:18
  180.7 7.6 %convert_reduce_fusion.3 = (f32[48,384]{1,0:T(8,128)}, f32[48,384]{1,0:T(8,128)}, bf16[32,48,384]{2,1,0:T(8,128)(2,1)S(1)}) fusion(bf16[32,48,384]{2,1,0:T(8,128)(2,1)S(1)} %get-tuple-element.34, bf16[32,384,384]{2,1,0:T(8,128)(2,1)} %all-gather.4.cloned.1.call-done), kind=kOutput, calls=%fused_computation.29 | convolution fusion | flops 455897088 | bytes 11943936 | tf_op jit(solution)/shard_map/cik,cjk->cij/dot_general | solution.py:15
  188.6 16.0 %all-reduce.7.cloned.1.call-done = (f32[48,384]{1,0:T(8,128)}, f32[48,384]{1,0:T(8,128)}) async-done(((f32[48,384]{1,0:T(8,128)}, f32[48,384]{1,0:T(8,128)}), (f32[48,384]{1,0:T(8,128)}, f32[48,384]{1,0:T(8,128)})) %all-reduce.7.cloned.1.call-update) | async-done | bytes 147472 | tf_op jit(solution)/shard_map/psum | solution.py:76
  206.0 4.5 fusion.40
  216.2 13.6 %reduce-scatter.3.cloned.1.call-done = f32[24,384,128]{2,1,0:T(8,128)} async-done(((f32[48,384,128]{2,1,0:T(8,128)}), f32[24,384,128]{2,1,0:T(8,128)}) %reduce-scatter.3.cloned.1.call-update) | async-done | bytes 4718608 | tf_op jit(solution)/shard_map/reduce_scatter | solution.py:84
  229.8 6.8 %add_convert_fusion.1 = bf16[24,384,128]{2,1,0:T(8,128)(2,1)} fusion(f32[24,384,128]{2,1,0:T(8,128)} %bitcast.122, f32[24,384,128]{2,1,0:T(8,128)} %reduce-scatter.3.cloned.1.call-done, bf16[48,384,128]{2,1,0:T(8,128)(2,1)} %param.8, s32[]{:T(128)S(6)} %select_n.4), kind=kLoop, calls=%fused_computation.23 | loop fusion | flops 4718592 | bytes 14155780 | tf_op jit(solution)/shard_map/convert_element_type | solution.py:90
  236.7 15.7 %all-gather.6.cloned.1.call-done = bf16[48,384,128]{2,1,0:T(8,128)(2,1)} async-done(((bf16[24,384,128]{2,1,0:T(8,128)(2,1)}), bf16[48,384,128]{2,1,0:T(8,128)(2,1)}) %all-gather.6.cloned.1.call-update) | async-done | bytes 4718608 | tf_op jit(solution)/shard_map/all_gather | solution.py:48
  252.4 6.3 %convert_reduce_fusion = (f32[48,384]{1,0:T(8,128)S(1)}, f32[48,384]{1,0:T(8,128)S(1)}) fusion(bf16[48,384,128]{2,1,0:T(8,128)(2,1)} %all-gather.6.cloned.1.call-done), kind=kLoop, calls=%fused_computation.2 | loop fusion | flops 9400320 | bytes 4866048 | tf_op jit(solution)/shard_map/reduce_sum | solution.py:8
  258.8 6.0 %fusion.12 = bf16[48,384,128]{2,1,0:T(8,128)(2,1)S(1)} fusion(bf16[48,384,128]{2,1,0:T(8,128)(2,1)S(1)} %copy-done.3, f32[128]{0:T(128)S(1)} %copy-done.11, f32[48,384]{1,0:T(8,128)S(1)} %get-tuple-element.30, f32[48,384]{1,0:T(8,128)S(1)} %get-tuple-element.29), kind=kLoop, calls=%fused_computation.20 | loop fusion | flops 11796480 | bytes 9585152 | tf_op jit(solution)/shard_map/convert_element_type | solution.py:51
  273.8 8.7 %all-reduce.5.cloned.1.call-start = ((), (), s32[]{:S(2)}) async-start(), calls=%async_computation.8 | async-start | bytes 294912 | tf_op jit(solution)/shard_map/psum | solution.py:76
  282.5 5.4 %copy.13 = bf16[32,48,384]{1,0,2:T(8,128)(2,1)S(1)} copy(bf16[32,48,384]{2,1,0:T(8,128)(2,1)} %get-tuple-element.28) | data formatting | bytes 2359296 | tf_op jit(solution)/shard_map/convert_element_type | solution.py:57
  287.8 6.0 %reshape.151 = bf16[8,2,36864]{2,1,0:T(2,128)(2,1)} reshape(bf16[384,32,48]{2,1,0:T(8,128)(2,1)S(1)} %bitcast.112) | data formatting | bytes 2359296
  293.9 57.9 %all_to_all.18 = bf16[8,2,36864]{2,1,0:T(2,128)(2,1)} all-to-all(bf16[8,2,36864]{2,1,0:T(2,128)(2,1)} %reshape.151), channel_id=1, replica_groups=mesh['groups'=2,'rows'=8,'chan'=2] {'rows'}, dimensions={0} | all-to-all | bytes 2359296 | tf_op jit(solution)/shard_map/all_to_all | solution.py:24
  351.7 4.3 reshape.152
  359.7 4.4 all_to_all.16
  364.1 72.7 %all-gather.8.cloned.1.call-done = bf16[32,384,384]{2,1,0:T(8,128)(2,1)} async-done(((bf16[32,48,384]{2,1,0:T(8,128)(2,1)}), bf16[32,384,384]{2,1,0:T(8,128)(2,1)}) %all-gather.8.cloned.1.call-update) | async-done | bytes 9437200 | tf_op jit(solution)/shard_map/all_gather | solution.py:28
  436.8 6.0 %convert_reduce_fusion.2 = (f32[48,384]{1,0:T(8,128)}, f32[48,384]{1,0:T(8,128)}, bf16[32,48,384]{2,1,0:T(8,128)(2,1)S(1)}) fusion(bf16[32,384,48]{1,2,0:T(8,128)(2,1)S(1)} %all_to_all.16, bf16[32,384,384]{2,1,0:T(8,128)(2,1)} %all-gather.8.cloned.1.call-done), kind=kOutput, calls=%fused_computation.26 | convolution fusion | flops 455897088 | bytes 11943936 | tf_op jit(solution)/shard_map/cki,ckj->cij/dot_general | solution.py:25
  442.9 16.3 %all-reduce.5.cloned.1.call-done = (f32[48,384]{1,0:T(8,128)}, f32[48,384]{1,0:T(8,128)}) async-done(((f32[48,384]{1,0:T(8,128)}, f32[48,384]{1,0:T(8,128)}), (f32[48,384]{1,0:T(8,128)}, f32[48,384]{1,0:T(8,128)})) %all-reduce.5.cloned.1.call-update) | async-done | bytes 147472 | tf_op jit(solution)/shard_map/psum | solution.py:76
  460.6 4.5 fusion.38
  470.5 13.8 %reduce-scatter.5.cloned.1.call-done = f32[24,384,128]{2,1,0:T(8,128)} async-done(((f32[48,384,128]{2,1,0:T(8,128)}), f32[24,384,128]{2,1,0:T(8,128)}) %reduce-scatter.5.cloned.1.call-update) | async-done | bytes 4718608 | tf_op jit(solution)/shard_map/reduce_scatter | solution.py:84
  484.3 6.8 %add_convert_fusion = bf16[24,384,128]{2,1,0:T(8,128)(2,1)} fusion(f32[24,384,128]{2,1,0:T(8,128)} %bitcast.121, f32[24,384,128]{2,1,0:T(8,128)} %reduce-scatter.5.cloned.1.call-done, bf16[48,384,128]{2,1,0:T(8,128)(2,1)} %all-gather.6.cloned.1.call-done, s32[]{:T(128)S(6)} %select_n.4), kind=kLoop, calls=%fused_computation.22 | loop fusion | flops 4718592 | bytes 14155780 | tf_op jit(solution)/shard_map/convert_element_type | solution.py:90
  (71 shorter events, 42.4 us)
Async XLA Ops:
  6.5 174.2 %all-gather.4.cloned.1.call-start = ((), (), s32[]{:S(2)}) async-start(), calls=%async_computation.3 | async-start | bytes 10616832 | tf_op jit(solution)/shard_map/all_gather | solution.py:18
  9.9 6.4 %copy-start.2 = (bf16[48,384,128]{2,1,0:T(8,128)(2,1)S(1)}, bf16[48,384,128]{2,1,0:T(8,128)(2,1)}, u32[]{:S(2)}) copy-start(bf16[48,384,128]{2,1,0:T(8,128)(2,1)} %param.8) | copy-start | bytes 14155780
  22.2 2.3 copy-start
  32.6 1.9 copy-start.7
  32.6 2.5 copy-start.4
  35.1 4.9 copy-start.5
  40.0 164.7 %all-reduce.7.cloned.1.call-start = ((), (), s32[]{:S(2)}) async-start(), calls=%async_computation.9 | async-start | bytes 294912 | tf_op jit(solution)/shard_map/psum | solution.py:76
  180.7 7.9 %copy-start.12 = (bf16[2,32]{1,0:T(2,128)(2,1)S(1)}, bf16[2,32]{1,0:T(2,128)(2,1)}, u32[]{:S(2)}) copy-start(bf16[2,32]{1,0:T(2,128)(2,1)} %param.14) | copy-start | bytes 388
  188.3 17.8 %copy-start.10 = (bf16[2,32,128]{2,1,0:T(8,128)(2,1)S(1)}, bf16[2,32,128]{2,1,0:T(8,128)(2,1)}, u32[]{:S(2)}) copy-start(bf16[2,32,128]{2,1,0:T(8,128)(2,1)} %param.15) | copy-start | bytes 49156
  188.3 41.5 %reduce-scatter.3.cloned.1.call-start = ((), (), s32[]{:S(2)}) async-start(), calls=%async_computation.4 | async-start | bytes 14155776 | tf_op jit(solution)/shard_map/reduce_scatter | solution.py:84
  210.6 41.8 %all-gather.6.cloned.1.call-start = ((), (), s32[]{:S(2)}) async-start(), calls=%async_computation.5 | async-start | bytes 7077888 | tf_op jit(solution)/shard_map/all_gather | solution.py:48
  210.7 1.9 copy-start.13
  236.6 22.1 %copy-start.11 = (f32[128]{0:T(128)S(1)}, f32[128]{0:T(128)}, u32[]{:S(2)}) copy-start(f32[128]{0:T(128)} %get-tuple-element.47) | copy-start | bytes 1540
  236.6 200.2 %all-gather.8.cloned.1.call-start = ((), (), s32[]{:S(2)}) async-start(), calls=%async_computation.6 | async-start | bytes 10616832 | tf_op jit(solution)/shard_map/all_gather | solution.py:28
  252.4 6.4 %copy-start.3 = (bf16[48,384,128]{2,1,0:T(8,128)(2,1)S(1)}, bf16[48,384,128]{2,1,0:T(8,128)(2,1)}, u32[]{:S(2)}) copy-start(bf16[48,384,128]{2,1,0:T(8,128)(2,1)} %all-gather.6.cloned.1.call-done) | copy-start | bytes 14155780
  258.7 8.1 %copy-start.8 = (bf16[128,32]{0,1:T(8,128)(2,1)S(1)}, bf16[128,32]{0,1:T(8,128)(2,1)}, u32[]{:S(2)}) copy-start(bf16[128,32]{0,1:T(8,128)(2,1)} %get-tuple-element.43) | copy-start | bytes 24580
  258.8 8.1 %copy-start.9 = (bf16[128,32]{0,1:T(8,128)(2,1)S(1)}, bf16[128,32]{0,1:T(8,128)(2,1)}, u32[]{:S(2)}) copy-start(bf16[128,32]{0,1:T(8,128)(2,1)} %get-tuple-element.44) | copy-start | bytes 24580
  264.7 2.1 copy-start.1
  270.8 0.9 copy-start.6
  273.8 185.4 %all-reduce.5.cloned.1.call-start = ((), (), s32[]{:S(2)}) async-start(), calls=%async_computation.8 | async-start | bytes 294912 | tf_op jit(solution)/shard_map/psum | solution.py:76
  442.8 41.5 %reduce-scatter.5.cloned.1.call-start = ((), (), s32[]{:S(2)}) async-start(), calls=%async_computation.7 | async-start | bytes 14155776 | tf_op jit(solution)/shard_map/reduce_scatter | solution.py:84
Sparse Core Ops, SparseCore 0:
  40.1 140.5 all-gather.3
  188.4 16.2 all-reduce.6
  210.7 19.0 reduce-scatter.2
  236.7 15.5 all-gather.5
  273.9 162.8 all-gather.7
  443.0 16.2 all-reduce.4
  465.3 19.0 reduce-scatter.4
where the time goes:
time: 508 us; the launch traced here: 498 us
  waiting for transfers between devices  289 us (57%)
  blocking collectives  57.9 us (11%)
  other arithmetic  51.7 us (10%)
  local copies, waits for them, and re-layouts  43.3 us (9%)
  matrix products  32.6 us (6%)
  between operations  14.6 us (3%)
  starting transfers between devices  9.13 us (2%)
    all_gather x1, waiting for transfers between devices, outgoing(): lax.all_gather(right_side, 'rows', axis=1, tiled=True)  141 us
    all_gather x1, waiting for transfers between devices, incoming(): lax.all_gather(right_side, 'rows', axis=1, tiled=True)  72.7 us
    all_to_all x1, blocking collectives, incoming(): lax.all_to_all(left_side, 'rows', split_axis=2, concat_axis=1, tiled=True)  57.9 us
    psum x2, waiting for transfers between devices, shards(): lax.psum((jnp.sum(values, axis=0), jnp.sum(values * values, axis=0)), 'ch...  32.4 us
    reduce_scatter x2, waiting for transfers between devices, shards(): lax.psum_scatter(jnp.einsum('cij,cd->ijd', scaled, out_weight, preferred_...  27.4 us
    unnamed x38, local copies, waits for them, and re-layouts  24.7 us
    all_gather x1, waiting for transfers between devices, shards(): current = lax.all_gather(current, 'chan', axis=0, tiled=True)  15.7 us
    convert_element_type x2, other arithmetic, shards(): (current_half.astype(jnp.float32) + gate_values * update).astype(jnp.bflo...  13.6 us
  transfers between devices with their start and end apart: 7, of which 7 were waited for; matrix products, arithmetic and copies ran while one was open for 6% of the time, Pallas kernels for 0%

commit v1 on v0

v1 whole, which is shorter than its diff:
```python
import functools

import jax
import jax.numpy as jnp
from jax import lax
from jax.experimental import pallas as pl
from jax.experimental.pallas import tpu as pltpu
from jax.sharding import PartitionSpec as P

F32 = jnp.float32
BF16 = jnp.bfloat16
NT = (((1,), (1,)), ((), ()))
TN = (((0,), (0,)), ((), ()))


def kernel(
    dims, pair_ref, weight_ref, pack_ref, gain_ref, gate_ref, out_ref,
    z, x, wfull, rows_f, left_f, right_f, prod_f, norm_f,
    send_lr, recv_lr, send_p, recv_p,
    local_sem, wsend_sem, wrecv_sem, send_sem, recv_sem,
):
    peers, cores, rows, rows_pad, cols, chans, own, feats = dims
    half = chans // cores
    core = lax.axis_index("chan")
    me = lax.axis_index("rows") * cores + core

    def peer_id(p):
        return {"rows": p // cores, "chan": p % cores}

    load = pltpu.make_async_copy(pair_ref.at[pl.ds(core * rows, rows)], z, local_sem.at[0])
    load.start()
    keep = pltpu.make_async_copy(pack_ref, wfull.at[core], local_sem.at[1])
    keep.start()

    barrier = pltpu.get_barrier_semaphore()

    @pl.loop(1, peers)
    def _(s):
        pl.semaphore_signal(
            barrier, inc=1, device_id=peer_id((me + s) % peers), device_id_type=pl.DeviceIdType.MESH
        )

    pl.semaphore_wait(barrier, peers - 1)

    share = pltpu.make_async_remote_copy(
        src_ref=pack_ref, dst_ref=wfull.at[core], send_sem=wsend_sem, recv_sem=wrecv_sem,
        device_id=peer_id(me - core + 1 - core), device_id_type=pl.DeviceIdType.MESH,
    )
    share.start()
    load.wait()
    keep.wait()
    share.wait()

    def exchange(phase, src, dst, p):
        return pltpu.make_async_remote_copy(
            src_ref=src.at[p], dst_ref=dst.at[me],
            send_sem=send_sem.at[phase, p], recv_sem=recv_sem.at[phase, me],
            device_id=peer_id(p), device_id_type=pl.DeviceIdType.MESH,
        )

    def arrived(phase, src, dst, p):
        return pltpu.make_async_remote_copy(
            src_ref=src.at[p], dst_ref=dst.at[p],
            send_sem=send_sem.at[phase, p], recv_sem=recv_sem.at[phase, p],
            device_id=peer_id(p), device_id_type=pl.DeviceIdType.MESH,
        )

    for u in range(2):
        gain_in = gain_ref[pl.ds(u, 1), :].astype(F32)
        to_lr, from_lr = send_lr.at[u], recv_lr.at[u]
        to_p, from_p = send_p.at[u], recv_p.at[u]

        @pl.loop(0, rows)
        def _(i):
            v = z[i].astype(F32)
            average = jnp.mean(v, axis=1, keepdims=True)
            squares = jnp.mean(v * v, axis=1, keepdims=True)
            spread = jnp.maximum(squares - average * average, 0.0)
            xb = ((v - average) * lax.rsqrt(spread + 1e-5) * gain_in).astype(BF16)
            x[i] = xb
            w = weight_ref[i]
            for h in range(cores):
                p_t = lax.dot_general(wfull[h, u, : 4 * half], xb, NT, preferred_element_type=F32)
                for lr in range(2):
                    g = p_t[2 * lr * half : (2 * lr + 1) * half]
                    val = p_t[(2 * lr + 1) * half : (2 * lr + 2) * half]
                    at = pl.multiple_of(i * (2 * chans) + (lr * chans + h * half), 8)
                    piece = w * jax.nn.sigmoid(g) * val
                    for t in range(cols // 128):
                        rows_f[t, pl.ds(at, half), :] = piece[:, t * 128 : (t + 1) * 128]

        def fill(p, target):
            for lr in range(2):
                for c in range(own):
                    for t in range(cols // 128):
                        target[lr, c, :, t * 128 : (t + 1) * 128] = rows_f[
                            t, pl.ds(lr * chans + p * own + c, rows, stride=2 * chans), :
                        ].astype(BF16)

        @pl.loop(1, peers)
        def _(s):
            p = (me + s) % peers
            fill(p, to_lr.at[p])
            exchange(2 * u, to_lr, from_lr, p).start()

        fill(me, from_lr.at[me])

        @pl.loop(1, peers)
        def _(s):
            p = (me + s) % peers
            arrived(2 * u, to_lr, from_lr, p).wait_recv()

        @pl.loop(0, own)
        def _(c):
            for p in range(peers):
                left_f[p * rows : (p + 1) * rows, :] = from_lr[p, 0, c].astype(F32)
                right_f[p * rows : (p + 1) * rows, :] = from_lr[p, 1, c].astype(F32)
            prod_f[...] = lax.dot_general(
                left_f[...].astype(BF16), right_f[...].astype(BF16), NT if u == 0 else TN,
                preferred_element_type=F32,
            )
            for p in range(peers):
                to_p[p, c] = prod_f[p * rows : (p + 1) * rows, :].astype(BF16)

        @pl.loop(1, peers)
        def _(s):
            exchange(2 * u + 1, to_p, from_p, (me + s) % peers).start()

        from_p[me] = to_p[me]

        @pl.loop(1, peers)
        def _(s):
            p = (me + s) % peers
            arrived(2 * u + 1, to_p, from_p, p).wait_recv()

        def add(p, sums):
            total, squares = sums
            for c in range(own):
                v = from_p[p, c].astype(F32)
                total, squares = total + v, squares + v * v
            return total, squares

        zero = jnp.zeros((rows, cols), F32)
        total, squares = lax.fori_loop(0, peers, add, (zero, zero))
        average = total / chans
        scale = lax.rsqrt(jnp.maximum(squares / chans - average * average, 0.0) + 1e-5)

        @pl.loop(0, peers)
        def _(p):
            for c in range(own):
                at = pl.multiple_of((p * own + c) * rows_pad, 8)
                piece = (from_p[p, c].astype(F32) - average) * scale
                for t in range(cols // 128):
                    norm_f[t, pl.ds(at, rows), :] = piece[:, t * 128 : (t + 1) * 128]

        w_out = jnp.concatenate(
            [wfull[h, u, 4 * half : 5 * half] for h in range(cores)], axis=0
        )
        gain_out = jnp.concatenate(
            [wfull[h, u, 5 * half : 6 * half] for h in range(cores)], axis=0
        ).astype(F32)
        w_gate = gate_ref[u]

        @pl.loop(0, rows)
        def _(i):
            scaled = jnp.concatenate(
                [
                    (norm_f[t, pl.ds(i, chans, stride=rows_pad), :] * gain_out).astype(BF16)
                    for t in range(cols // 128)
                ],
                axis=1,
            )
            update = lax.dot_general(scaled, w_out, TN, preferred_element_type=F32)
            gate = jax.nn.sigmoid(jnp.dot(x[i], w_gate, preferred_element_type=F32))
            result = (z[i].astype(F32) + gate * update).astype(BF16)
            if u == 0:
                z[i] = result
            else:
                out_ref[i] = result

    for u in range(2):

        @pl.loop(1, peers)
        def _(s):
            p = (me + s) % peers
            arrived(2 * u, send_lr.at[u], recv_lr.at[u], p).wait_send()
            arrived(2 * u + 1, send_p.at[u], recv_p.at[u], p).wait_send()


def shards(pair, seq_len, pair_mask, ln_in_gain, w_proj, w_gate, ln_out_gain, w_out):
    rows_chip, cols, feats = pair.shape
    cores = lax.axis_size("chan")
    peers = lax.axis_size("rows") * cores
    rows = rows_chip // cores
    rows_pad = -(-rows // 8) * 8
    half = w_proj.shape[3]
    chans = half * cores
    own = chans // peers
    first = (lax.axis_index("rows") * cores + lax.axis_index("chan")) * rows
    valid = (jnp.arange(cols) < seq_len[0]).astype(F32)
    mask = lax.dynamic_slice_in_dim(pair_mask, lax.axis_index("chan") * rows, rows, 0)
    weight = (
        mask.astype(F32) * lax.dynamic_slice_in_dim(valid, first, rows)[:, None] * valid[None, :]
    )[:, None, :]
    pack = jnp.concatenate(
        [
            w_proj.transpose(0, 1, 3, 2).reshape(2, 4 * half, feats),
            w_out,
            jnp.broadcast_to(ln_out_gain[:, :, None], (2, half, feats)),
        ],
        axis=1,
    )
    dims = (peers, cores, rows, rows_pad, cols, chans, own, feats)
    tiles = cols // 128
    vmem = pl.BlockSpec(memory_space=pltpu.VMEM)
    return pl.pallas_call(
        functools.partial(kernel, dims),
        out_shape=jax.ShapeDtypeStruct((rows, cols, feats), BF16),
        in_specs=[pl.BlockSpec(memory_space=pl.ANY), vmem, vmem, vmem, vmem],
        out_specs=vmem,
        scratch_shapes=[
            pltpu.VMEM((rows, cols, feats), BF16),
            pltpu.VMEM((rows, cols, feats), BF16),
            pltpu.VMEM((cores,) + pack.shape, BF16),
            pltpu.VMEM((tiles, rows * 2 * chans, 128), F32),
            pltpu.VMEM((cols, cols), F32),
            pltpu.VMEM((cols, cols), F32),
            pltpu.VMEM((cols, cols), F32),
            pltpu.VMEM((tiles, chans * rows_pad, 128), F32),
            pltpu.VMEM((2, peers, 2, own, rows, cols), BF16),
            pltpu.VMEM((2, peers, 2, own, rows, cols), BF16),
            pltpu.VMEM((2, peers, own, rows, cols), BF16),
            pltpu.VMEM((2, peers, own, rows, cols), BF16),
            pltpu.SemaphoreType.DMA((2,)),
            pltpu.SemaphoreType.DMA,
            pltpu.SemaphoreType.DMA,
            pltpu.SemaphoreType.DMA((4, peers)),
            pltpu.SemaphoreType.DMA((4, peers)),
        ],
        compiler_params=pltpu.CompilerParams(
            collective_id=0, has_side_effects=True, vmem_limit_bytes=60 * 1024 * 1024
        ),
        name="triangle",
    )(pair, weight, pack, ln_in_gain, w_gate)


def solution(mesh):
    in_specs = (
        P(("groups", "rows"), None, None),
        P("groups"),
        P(("groups", "rows"), None),
        P(),
        P(None, None, None, "chan"),
        P(),
        P(None, "chan"),
        P(None, "chan", None),
    )
    out_specs = P(("groups", "rows", "chan"), None, None)
    return jax.shard_map(shards, mesh=mesh, in_specs=in_specs, out_specs=out_specs, check_vma=False)
```

time: 508 us -> 216 us (0.43)
  the two profiles are of different devices: /device:TPU:0 before, /device:TPU:21 now
where the time goes in v1:
time: 216 us; the launch traced here: 215 us
  Pallas kernels  208 us (96%)
  local copies, waits for them, and re-layouts  4.74 us (2%)
  other arithmetic  2.35 us (1%)
    pallas_call x1, Pallas kernels, shards(): pl.pallas_call(functools.partial(kernel, dims), out_shape=jax.ShapeDtypeS...  208 us

profile of v1, /device:TPU:21, one launch (start us, length us, event | category | flops | bytes accessed | tf_op | source)
XLA Modules:
  0.0 215.3 jit_solution(988932371249940569)
XLA Ops:
  0.7 0.1 dynamic_slice.7
  0.7 0.7 broadcast_in_dim.5
  1.5 0.8 multiply_multiply_fusion
  2.3 0.6 broadcast_in_dim.4.weight_ref
  2.9 1.5 pad_maximum_fusion.pack_ref
  4.5 207.5 %triangle.1 = bf16[24,384,128]{2,1,0:T(8,128)(2,1)} custom-call(bf16[48,384,128]{2,1,0:T(8,128)(2,1)} %pair_ref.1, f32[24,1,384]{2,1,0:T(1,128)} %broadcast_in_dim.4.weight_ref, bf16[2,192,128]{2,1,0:T(8,128)(2,1)} %pad_maximum_fusion.pack_ref, bf16[2,128]{1,0:T(2,128)(2,1)} %gain_ref.1, bf16[2,128,128]{2,1,0:T(8,128)(2,1)} %gate_ref.1), custom_call_target="tpu_custom_call" | custom-call | tf_op jit(solution)/shard_map/triangle/pallas_call | solution.py:216
  212.0 3.3 %copy.11 = bf16[24,384,128]{2,1,0:T(8,128)(2,1)} copy(bf16[24,384,128]{2,1,0:T(8,128)(2,1)} %triangle.1) | data formatting | bytes 4718592
  (1 shorter events, 0.0 us)

commit v2 on v1

v2 whole, which is shorter than its diff:
```python
import functools

import jax
import jax.numpy as jnp
from jax import lax
from jax.experimental import pallas as pl
from jax.experimental.pallas import tpu as pltpu
from jax.sharding import PartitionSpec as P

F32 = jnp.float32
BF16 = jnp.bfloat16
NT = (((1,), (1,)), ((), ()))
TN = (((0,), (0,)), ((), ()))


def kernel(
    dims, pair_ref, weight_ref, pack_ref, gain_ref, gate_ref, out_ref,
    z, x, wfull, rows_f, left_f, right_f, prod_f, norm_f,
    send_lr, recv_lr, recv_far, send_p, recv_p, send_q, recv_q,
    local_sem, wsend_sem, wrecv_sem, send_sem, recv_sem,
):
    slots, cores, rows, rows_pad, cols, chans, own, feats = dims
    peers = 2 * slots
    half = chans // cores
    slots_core = slots // cores
    core = lax.axis_index("chan")
    me = lax.axis_index("rows") * cores + core
    side = me // slots
    slot = me % slots

    def device(p):
        return {"rows": p // cores, "chan": p % cores}

    load = pltpu.make_async_copy(pair_ref.at[pl.ds(core * rows, rows)], z, local_sem.at[0])
    load.start()
    keep = pltpu.make_async_copy(pack_ref, wfull.at[core], local_sem.at[1])
    keep.start()

    barrier = pltpu.get_barrier_semaphore()

    @pl.loop(1, peers)
    def _(s):
        pl.semaphore_signal(
            barrier, inc=1, device_id=device((me + s) % peers), device_id_type=pl.DeviceIdType.MESH
        )

    pl.semaphore_wait(barrier, peers - 1)

    share = pltpu.make_async_remote_copy(
        src_ref=pack_ref, dst_ref=wfull.at[core], send_sem=wsend_sem, recv_sem=wrecv_sem,
        device_id=device(me - core + 1 - core), device_id_type=pl.DeviceIdType.MESH,
    )
    share.start()
    load.wait()

    def send(phase, src, dst, far, q):
        return pltpu.make_async_remote_copy(
            src_ref=src, dst_ref=dst.at[slot],
            send_sem=send_sem.at[phase, q], recv_sem=recv_sem.at[phase, slot],
            device_id=device((1 - side if far else side) * slots + q),
            device_id_type=pl.DeviceIdType.MESH,
        )

    def arrival(phase, src, dst, far, q):
        return pltpu.make_async_remote_copy(
            src_ref=src, dst_ref=dst.at[q],
            send_sem=send_sem.at[phase, q], recv_sem=recv_sem.at[phase, q],
            device_id=device((1 - side if far else side) * slots + q),
            device_id_type=pl.DeviceIdType.MESH,
        )

    def normalize_rows(u):
        gain_in = gain_ref[pl.ds(u, 1), :].astype(F32)

        @pl.loop(0, rows)
        def _(i):
            v = z[i].astype(F32)
            average = jnp.mean(v, axis=1, keepdims=True)
            squares = jnp.mean(v * v, axis=1, keepdims=True)
            spread = jnp.maximum(squares - average * average, 0.0)
            x[i] = ((v - average) * lax.rsqrt(spread + 1e-5) * gain_in).astype(BF16)

    def project(u, h):
        @pl.loop(0, rows)
        def _(i):
            w = weight_ref[i]
            p_t = lax.dot_general(wfull[h, u, : 4 * half], x[i], NT, preferred_element_type=F32)
            for lr in range(2):
                g = p_t[2 * lr * half : (2 * lr + 1) * half]
                val = p_t[(2 * lr + 1) * half : (2 * lr + 2) * half]
                at = pl.multiple_of(i * (2 * half) + lr * half, 8)
                piece = w * jax.nn.sigmoid(g) * val
                for t in range(cols // 128):
                    rows_f[t, pl.ds(at, half), :] = piece[:, t * 128 : (t + 1) * 128]

    def fill(q, target):
        for lr in range(2):
            for c in range(own):
                for t in range(cols // 128):
                    target[lr, c, :, t * 128 : (t + 1) * 128] = rows_f[
                        t, pl.ds(lr * half + q * own + c, rows, stride=2 * half), :
                    ].astype(BF16)

    for u in range(2):
        to_lr, from_lr = send_lr.at[u], recv_lr.at[u]
        near = 3 * u
        normalize_rows(u)
        if u == 0:
            keep.wait()
            share.wait()

        for turn in range(cores):
            h = (slot // slots_core + 1 + turn) % cores
            project(u, h)

            @pl.loop(0, slots_core)
            def _(s):
                r = (slot + s) % slots_core
                q = h * slots_core + r
                fill(r, to_lr.at[q])
                if u == 0:
                    send(1, to_lr.at[q, 1], recv_far, True, q).start()

                @pl.when(q != slot)
                def _():
                    send(near, to_lr.at[q], from_lr, False, q).start()

        from_lr[slot] = to_lr[slot]

        @pl.loop(1, slots)
        def _(s):
            q = (slot + s) % slots
            arrival(near, to_lr.at[q], from_lr, False, q).wait_recv()

        if u == 0:

            @pl.loop(0, slots)
            def _(q):
                arrival(1, to_lr.at[q, 1], recv_far, True, q).wait_recv()

            @pl.loop(0, own)
            def _(c):
                for q in range(slots):
                    at = pl.ds(q * rows, rows)
                    left_f[at, :] = from_lr[q, 0, c].astype(F32)
                    right_f[side, at, :] = from_lr[q, 1, c].astype(F32)
                    right_f[1 - side, at, :] = recv_far[q, c].astype(F32)
                right = right_f[...].reshape(cols, cols).astype(BF16)
                prod_f[0] = lax.dot_general(
                    left_f[...].astype(BF16), right, NT, preferred_element_type=F32
                )
                for q in range(slots):
                    send_p[q, c] = prod_f[0, q * rows : (q + 1) * rows, :].astype(BF16)

            @pl.loop(1, slots)
            def _(s):
                q = (slot + s) % slots
                send(2, send_p.at[q], recv_p, False, q).start()

            recv_p[slot] = send_p[slot]

            @pl.loop(1, slots)
            def _(s):
                q = (slot + s) % slots
                arrival(2, send_p.at[q], recv_p, False, q).wait_recv()

        else:

            @pl.loop(0, own)
            def _(c):
                for q in range(slots):
                    at = pl.ds(q * rows, rows)
                    left_f[at, :] = from_lr[q, 0, c].astype(F32)
                    right_f[0, at, :] = from_lr[q, 1, c].astype(F32)
                prod_f[...] = lax.dot_general(
                    left_f[...].astype(BF16), right_f[0].astype(BF16), TN,
                    preferred_element_type=F32,
                ).reshape(2, cols // 2, cols)
                for e in range(2):
                    for q in range(slots):
                        send_q[e, q, c] = prod_f[e, q * rows : (q + 1) * rows, :].astype(BF16)

            @pl.loop(0, slots)
            def _(s):
                q = (slot + s) % slots
                send(5, send_q.at[1 - side, q], recv_q.at[1], True, q).start()

                @pl.when(q != slot)
                def _():
                    send(4, send_q.at[side, q], recv_q.at[0], False, q).start()

            recv_q[0, slot] = send_q[side, slot]

            @pl.loop(0, slots)
            def _(q):
                @pl.when(q != slot)
                def _():
                    arrival(4, send_q.at[side, q], recv_q.at[0], False, q).wait_recv()

                arrival(5, send_q.at[1 - side, q], recv_q.at[1], True, q).wait_recv()
                for c in range(own):
                    recv_p[q, c] = (
                        recv_q[0, q, c].astype(F32) + recv_q[1, q, c].astype(F32)
                    ).astype(BF16)

        def add(q, sums):
            total, squares = sums
            for c in range(own):
                v = recv_p[q, c].astype(F32)
                total, squares = total + v, squares + v * v
            return total, squares

        zero = jnp.zeros((rows, cols), F32)
        total, squares = lax.fori_loop(0, slots, add, (zero, zero))
        average = total / chans
        scale = lax.rsqrt(jnp.maximum(squares / chans - average * average, 0.0) + 1e-5)

        @pl.loop(0, slots)
        def _(q):
            for c in range(own):
                at = pl.multiple_of((q * own + c) * rows_pad, 8)
                piece = (recv_p[q, c].astype(F32) - average) * scale
                for t in range(cols // 128):
                    norm_f[t, pl.ds(at, rows), :] = piece[:, t * 128 : (t + 1) * 128]

        w_out = jnp.concatenate(
            [wfull[h, u, 4 * half : 5 * half] for h in range(cores)], axis=0
        )
        gain_out = jnp.concatenate(
            [wfull[h, u, 5 * half : 6 * half] for h in range(cores)], axis=0
        ).astype(F32)
        w_gate = gate_ref[u]

        @pl.loop(0, rows)
        def _(i):
            scaled = jnp.concatenate(
                [
                    (norm_f[t, pl.ds(i, chans, stride=rows_pad), :] * gain_out).astype(BF16)
                    for t in range(cols // 128)
                ],
                axis=1,
            )
            update = lax.dot_general(scaled, w_out, TN, preferred_element_type=F32)
            gate = jax.nn.sigmoid(jnp.dot(x[i], w_gate, preferred_element_type=F32))
            result = (z[i].astype(F32) + gate * update).astype(BF16)
            if u == 0:
                z[i] = result
            else:
                out_ref[i] = result

    @pl.loop(0, slots)
    def _(q):
        arrival(1, send_lr.at[0, q, 1], recv_far, True, q).wait_send()
        arrival(5, send_q.at[1 - side, q], recv_q.at[1], True, q).wait_send()

        @pl.when(q != slot)
        def _():
            arrival(0, send_lr.at[0, q], recv_lr.at[0], False, q).wait_send()
            arrival(2, send_p.at[q], recv_p, False, q).wait_send()
            arrival(3, send_lr.at[1, q], recv_lr.at[1], False, q).wait_send()
            arrival(4, send_q.at[side, q], recv_q.at[0], False, q).wait_send()


def shards(pair, seq_len, pair_mask, ln_in_gain, w_proj, w_gate, ln_out_gain, w_out):
    rows_chip, cols, feats = pair.shape
    cores = lax.axis_size("chan")
    slots = lax.axis_size("rows") * cores // 2
    rows = rows_chip // cores
    rows_pad = -(-rows // 8) * 8
    half = w_proj.shape[3]
    chans = half * cores
    own = chans // slots
    first = (lax.axis_index("rows") * cores + lax.axis_index("chan")) * rows
    valid = (jnp.arange(cols) < seq_len[0]).astype(F32)
    mask = lax.dynamic_slice_in_dim(pair_mask, lax.axis_index("chan") * rows, rows, 0)
    weight = (
        mask.astype(F32) * lax.dynamic_slice_in_dim(valid, first, rows)[:, None] * valid[None, :]
    )[:, None, :]
    pack = jnp.concatenate(
        [
            w_proj.transpose(0, 1, 3, 2).reshape(2, 4 * half, feats),
            w_out,
            jnp.broadcast_to(ln_out_gain[:, :, None], (2, half, feats)),
        ],
        axis=1,
    )
    dims = (slots, cores, rows, rows_pad, cols, chans, own, feats)
    tiles = cols // 128
    vmem = pl.BlockSpec(memory_space=pltpu.VMEM)
    return pl.pallas_call(
        functools.partial(kernel, dims),
        out_shape=jax.ShapeDtypeStruct((rows, cols, feats), BF16),
        in_specs=[pl.BlockSpec(memory_space=pl.ANY), vmem, vmem, vmem, vmem],
        out_specs=vmem,
        scratch_shapes=[
            pltpu.VMEM((rows, cols, feats), BF16),
            pltpu.VMEM((rows, cols, feats), BF16),
            pltpu.VMEM((cores,) + pack.shape, BF16),
            pltpu.VMEM((tiles, rows * 2 * half, 128), F32),
            pltpu.VMEM((cols // 2, cols), F32),
            pltpu.VMEM((2, cols // 2, cols), F32),
            pltpu.VMEM((2, cols // 2, cols), F32),
            pltpu.VMEM((tiles, chans * rows_pad, 128), F32),
            pltpu.VMEM((2, slots, 2, own, rows, cols), BF16),
            pltpu.VMEM((2, slots, 2, own, rows, cols), BF16),
            pltpu.VMEM((slots, own, rows, cols), BF16),
            pltpu.VMEM((slots, own, rows, cols), BF16),
            pltpu.VMEM((slots, own, rows, cols), BF16),
            pltpu.VMEM((2, slots, own, rows, cols), BF16),
            pltpu.VMEM((2, slots, own, rows, cols), BF16),
            pltpu.SemaphoreType.DMA((2,)),
            pltpu.SemaphoreType.DMA,
            pltpu.SemaphoreType.DMA,
            pltpu.SemaphoreType.DMA((6, slots)),
            pltpu.SemaphoreType.DMA((6, slots)),
        ],
        compiler_params=pltpu.CompilerParams(
            collective_id=0, has_side_effects=True, vmem_limit_bytes=60 * 1024 * 1024
        ),
        name="triangle",
    )(pair, weight, pack, ln_in_gain, w_gate)


def solution(mesh):
    in_specs = (
        P(("groups", "rows"), None, None),
        P("groups"),
        P(("groups", "rows"), None),
        P(),
        P(None, None, None, "chan"),
        P(),
        P(None, "chan"),
        P(None, "chan", None),
    )
    out_specs = P(("groups", "rows", "chan"), None, None)
    return jax.shard_map(shards, mesh=mesh, in_specs=in_specs, out_specs=out_specs, check_vma=False)
```

time: 216 us -> 203 us (0.940)
  the two profiles are of different devices: /device:TPU:21 before, /device:TPU:0 now
where the time goes in v2:
time: 203 us
  Pallas kernels  195 us (96%)
  local copies, waits for them, and re-layouts  4.74 us (2%)
  other arithmetic  2.35 us (1%)
    pallas_call x1, Pallas kernels, shards(): pl.pallas_call(functools.partial(kernel, dims), out_shape=jax.ShapeDtypeS...  195 us

profile of v2, /device:TPU:0, one launch (start us, length us, event | category | flops | bytes accessed | tf_op | source)
XLA Modules:
  0.0 203.0 jit_solution(14578144534207808560)
XLA Ops:
  0.7 0.1 dynamic_slice.7
  0.7 0.7 broadcast_in_dim.5
  1.5 0.8 multiply_multiply_fusion
  2.3 0.6 broadcast_in_dim.4.weight_ref
  2.9 1.5 pad_maximum_fusion.pack_ref
  4.5 195.2 %triangle.1 = bf16[24,384,128]{2,1,0:T(8,128)(2,1)} custom-call(bf16[48,384,128]{2,1,0:T(8,128)(2,1)} %pair_ref.1, f32[24,1,384]{2,1,0:T(1,128)} %broadcast_in_dim.4.weight_ref, bf16[2,192,128]{2,1,0:T(8,128)(2,1)} %pad_maximum_fusion.pack_ref, bf16[2,128]{1,0:T(2,128)(2,1)} %gain_ref.1, bf16[2,128,128]{2,1,0:T(8,128)(2,1)} %gate_ref.1), custom_call_target="tpu_custom_call" | custom-call | tf_op jit(solution)/shard_map/triangle/pallas_call | solution.py:290
  199.7 3.3 %copy.11 = bf16[24,384,128]{2,1,0:T(8,128)(2,1)} copy(bf16[24,384,128]{2,1,0:T(8,128)(2,1)} %triangle.1) | data formatting | bytes 4718592
  (1 shorter events, 0.0 us)

commit v3 on v2

--- a/solution.py
+++ b/solution.py
@@ -15,14 +15,16 @@
 
 def kernel(
     dims, pair_ref, weight_ref, pack_ref, gain_ref, gate_ref, out_ref,
-    z, x, wfull, rows_f, left_f, right_f, prod_f, norm_f,
+    z, x, gates, wfull, rows_f, left_f, right_f, prod_f, norm_f,
     send_lr, recv_lr, recv_far, send_p, recv_p, send_q, recv_q,
-    local_sem, wsend_sem, wrecv_sem, send_sem, recv_sem,
+    local_sem, wsend_sem, wrecv_sem, send_sem, recv_sem, part_send, part_recv,
 ):
     slots, cores, rows, rows_pad, cols, chans, own, feats = dims
     peers = 2 * slots
     half = chans // cores
     slots_core = slots // cores
+    part = 2
+    parts = own // part
     core = lax.axis_index("chan")
     me = lax.axis_index("rows") * cores + core
     side = me // slots
@@ -65,6 +67,19 @@
         return pltpu.make_async_remote_copy(
             src_ref=src, dst_ref=dst.at[q],
             send_sem=send_sem.at[phase, q], recv_sem=recv_sem.at[phase, q],
+            device_id=device((1 - side if far else side) * slots + q),
+            device_id_type=pl.DeviceIdType.MESH,
+        )
+
+    def part_copy(phase, src, dst, far, q, g, to):
+        at = pl.ds(g * part, part)
+        if phase == 0:
+            src, dst = src.at[:, at], dst.at[to, :, at]
+        else:
+            src, dst = src.at[at], dst.at[to, at]
+        return pltpu.make_async_remote_copy(
+            src_ref=src, dst_ref=dst,
+            send_sem=part_send.at[phase, g, q], recv_sem=part_recv.at[phase, g, to],
             device_id=device((1 - side if far else side) * slots + q),
             device_id_type=pl.DeviceIdType.MESH,
         )
@@ -103,7 +118,6 @@
 
     for u in range(2):
         to_lr, from_lr = send_lr.at[u], recv_lr.at[u]
-        near = 3 * u
         normalize_rows(u)
         if u == 0:
             keep.wait()
@@ -121,18 +135,39 @@
                 if u == 0:
                     send(1, to_lr.at[q, 1], recv_far, True, q).start()
 
-                @pl.when(q != slot)
-                def _():
-                    send(near, to_lr.at[q], from_lr, False, q).start()
+                    @pl.when(q != slot)
+                    def _():
+                        send(0, to_lr.at[q], from_lr, False, q).start()
+
+            if u == 1:
+
+                @pl.loop(0, parts)
+                def _(g):
+                    @pl.loop(0, slots_core)
+                    def _(s):
+                        q = h * slots_core + (slot + s) % slots_core
+
+                        @pl.when(q != slot)
+                        def _():
+                            part_copy(0, to_lr.at[q], from_lr, False, q, g, slot).start()
 
         from_lr[slot] = to_lr[slot]
-
-        @pl.loop(1, slots)
-        def _(s):
-            q = (slot + s) % slots
-            arrival(near, to_lr.at[q], from_lr, False, q).wait_recv()
+        w_gate = gate_ref[u]
+
+        def open_gates(first, count):
+            @pl.loop(0, count)
+            def _(j):
+                gates[first + j] = jax.nn.sigmoid(
+                    jnp.dot(x[first + j], w_gate, preferred_element_type=F32)
+                )
 
         if u == 0:
+            open_gates(0, rows)
+
+            @pl.loop(1, slots)
+            def _(s):
+                q = (slot + s) % slots
+                arrival(0, to_lr.at[q], from_lr, False, q).wait_recv()
 
             @pl.loop(0, slots)
             def _(q):
@@ -166,42 +201,54 @@
 
         else:
 
-            @pl.loop(0, own)
-            def _(c):
-                for q in range(slots):
-                    at = pl.ds(q * rows, rows)
-                    left_f[at, :] = from_lr[q, 0, c].astype(F32)
-                    right_f[0, at, :] = from_lr[q, 1, c].astype(F32)
-                prod_f[...] = lax.dot_general(
-                    left_f[...].astype(BF16), right_f[0].astype(BF16), TN,
-                    preferred_element_type=F32,
-                ).reshape(2, cols // 2, cols)
-                for e in range(2):
+            @pl.loop(0, parts)
+            def _(g):
+                @pl.loop(1, slots)
+                def _(s):
+                    q = (slot + s) % slots
+                    part_copy(0, to_lr.at[q], from_lr, False, q, g, q).wait_recv()
+
+                @pl.loop(0, part)
+                def _(d):
+                    c = g * part + d
                     for q in range(slots):
-                        send_q[e, q, c] = prod_f[e, q * rows : (q + 1) * rows, :].astype(BF16)
-
-            @pl.loop(0, slots)
-            def _(s):
-                q = (slot + s) % slots
-                send(5, send_q.at[1 - side, q], recv_q.at[1], True, q).start()
-
-                @pl.when(q != slot)
-                def _():
-                    send(4, send_q.at[side, q], recv_q.at[0], False, q).start()
+                        at = pl.ds(q * rows, rows)
+                        left_f[at, :] = from_lr[q, 0, c].astype(F32)
+                        right_f[0, at, :] = from_lr[q, 1, c].astype(F32)
+                    prod_f[...] = lax.dot_general(
+                        left_f[...].astype(BF16), right_f[0].astype(BF16), TN,
+                        preferred_element_type=F32,
+                    ).reshape(2, cols // 2, cols)
+                    for e in range(2):
+                        for q in range(slots):
+                            send_q[e, q, c] = prod_f[e, q * rows : (q + 1) * rows, :].astype(BF16)
+
+                @pl.loop(0, slots)
+                def _(s):
+                    q = (slot + s) % slots
+                    part_copy(2, send_q.at[1 - side, q], recv_q.at[1], True, q, g, slot).start()
+
+                    @pl.when(q != slot)
+                    def _():
+                        part_copy(1, send_q.at[side, q], recv_q.at[0], False, q, g, slot).start()
 
             recv_q[0, slot] = send_q[side, slot]
-
-            @pl.loop(0, slots)
-            def _(q):
-                @pl.when(q != slot)
-                def _():
-                    arrival(4, send_q.at[side, q], recv_q.at[0], False, q).wait_recv()
-
-                arrival(5, send_q.at[1 - side, q], recv_q.at[1], True, q).wait_recv()
-                for c in range(own):
-                    recv_p[q, c] = (
-                        recv_q[0, q, c].astype(F32) + recv_q[1, q, c].astype(F32)
-                    ).astype(BF16)
+            open_gates(0, rows)
+
+            @pl.loop(0, parts)
+            def _(g):
+                @pl.loop(0, slots)
+                def _(q):
+                    @pl.when(q != slot)
+                    def _():
+                        part_copy(1, send_q.at[side, q], recv_q.at[0], False, q, g, q).wait_recv()
+
+                    part_copy(2, send_q.at[1 - side, q], recv_q.at[1], True, q, g, q).wait_recv()
+                    for d in range(part):
+                        c = g * part + d
+                        recv_p[q, c] = (
+                            recv_q[0, q, c].astype(F32) + recv_q[1, q, c].astype(F32)
+                        ).astype(BF16)
 
         def add(q, sums):
             total, squares = sums
@@ -229,7 +276,6 @@
         gain_out = jnp.concatenate(
             [wfull[h, u, 5 * half : 6 * half] for h in range(cores)], axis=0
         ).astype(F32)
-        w_gate = gate_ref[u]
 
         @pl.loop(0, rows)
         def _(i):
@@ -241,8 +287,7 @@
                 axis=1,
             )
             update = lax.dot_general(scaled, w_out, TN, preferred_element_type=F32)
-            gate = jax.nn.sigmoid(jnp.dot(x[i], w_gate, preferred_element_type=F32))
-            result = (z[i].astype(F32) + gate * update).astype(BF16)
+            result = (z[i].astype(F32) + gates[i] * update).astype(BF16)
             if u == 0:
                 z[i] = result
             else:
@@ -251,14 +296,20 @@
     @pl.loop(0, slots)
     def _(q):
         arrival(1, send_lr.at[0, q, 1], recv_far, True, q).wait_send()
-        arrival(5, send_q.at[1 - side, q], recv_q.at[1], True, q).wait_send()
 
         @pl.when(q != slot)
         def _():
             arrival(0, send_lr.at[0, q], recv_lr.at[0], False, q).wait_send()
             arrival(2, send_p.at[q], recv_p, False, q).wait_send()
-            arrival(3, send_lr.at[1, q], recv_lr.at[1], False, q).wait_send()
-            arrival(4, send_q.at[side, q], recv_q.at[0], False, q).wait_send()
+
+        @pl.loop(0, parts)
+        def _(g):
+            part_copy(2, send_q.at[1 - side, q], recv_q.at[1], True, q, g, q).wait_send()
+
+            @pl.when(q != slot)
+            def _():
+                part_copy(0, send_lr.at[1, q], recv_lr.at[1], False, q, g, q).wait_send()
+                part_copy(1, send_q.at[side, q], recv_q.at[0], False, q, g, q).wait_send()
 
 
 def shards(pair, seq_len, pair_mask, ln_in_gain, w_proj, w_gate, ln_out_gain, w_out):
@@ -295,6 +346,7 @@
         scratch_shapes=[
             pltpu.VMEM((rows, cols, feats), BF16),
             pltpu.VMEM((rows, cols, feats), BF16),
+            pltpu.VMEM((rows, cols, feats), F32),
             pltpu.VMEM((cores,) + pack.shape, BF16),
             pltpu.VMEM((tiles, rows * 2 * half, 128), F32),
             pltpu.VMEM((cols // 2, cols), F32),
@@ -311,8 +363,10 @@
             pltpu.SemaphoreType.DMA((2,)),
             pltpu.SemaphoreType.DMA,
             pltpu.SemaphoreType.DMA,
-            pltpu.SemaphoreType.DMA((6, slots)),
-            pltpu.SemaphoreType.DMA((6, slots)),
+            pltpu.SemaphoreType.DMA((3, slots)),
+            pltpu.SemaphoreType.DMA((3, slots)),
+            pltpu.SemaphoreType.DMA((3, own // 2, slots)),
+            pltpu.SemaphoreType.DMA((3, own // 2, slots)),
         ],
         compiler_params=pltpu.CompilerParams(
             collective_id=0, has_side_effects=True, vmem_limit_bytes=60 * 1024 * 1024

time: 203 us -> 190 us (0.936)
  Pallas kernels: 195 us -> 182 us
    pallas_call x1, Pallas kernels: 195 us -> 182 us  [shards(): pl.pallas_call(functools.partial(kernel, dims), out_shape=jax.ShapeDtypeS...]
where the time goes in v3:
time: 190 us
  Pallas kernels  182 us (96%)
  local copies, waits for them, and re-layouts  4.74 us (2%)
  other arithmetic  2.35 us (1%)
    pallas_call x1, Pallas kernels, shards(): pl.pallas_call(functools.partial(kernel, dims), out_shape=jax.ShapeDtypeS...  182 us

profile of v3, /device:TPU:0, one launch (start us, length us, event | category | flops | bytes accessed | tf_op | source)
XLA Modules:
  0.0 189.6 jit_solution(11821497219494595071)
XLA Ops:
  0.7 0.1 dynamic_slice.7
  0.7 0.7 broadcast_in_dim.5
  1.5 0.8 multiply_multiply_fusion
  2.3 0.6 broadcast_in_dim.4.weight_ref
  2.9 1.5 pad_maximum_fusion.pack_ref
  4.5 181.8 %triangle.1 = bf16[24,384,128]{2,1,0:T(8,128)(2,1)} custom-call(bf16[48,384,128]{2,1,0:T(8,128)(2,1)} %pair_ref.1, f32[24,1,384]{2,1,0:T(1,128)} %broadcast_in_dim.4.weight_ref, bf16[2,192,128]{2,1,0:T(8,128)(2,1)} %pad_maximum_fusion.pack_ref, bf16[2,128]{1,0:T(2,128)(2,1)} %gain_ref.1, bf16[2,128,128]{2,1,0:T(8,128)(2,1)} %gate_ref.1), custom_call_target="tpu_custom_call" | custom-call | tf_op jit(solution)/shard_map/triangle/pallas_call | solution.py:341
  186.3 3.3 %copy.11 = bf16[24,384,128]{2,1,0:T(8,128)(2,1)} copy(bf16[24,384,128]{2,1,0:T(8,128)(2,1)} %triangle.1) | data formatting | bytes 4718592
  (1 shorter events, 0.0 us)

commit v4 on v3

--- a/solution.py
+++ b/solution.py
@@ -87,7 +87,7 @@
     def normalize_rows(u):
         gain_in = gain_ref[pl.ds(u, 1), :].astype(F32)
 
-        @pl.loop(0, rows)
+        @pl.loop(0, rows, unroll=6)
         def _(i):
             v = z[i].astype(F32)
             average = jnp.mean(v, axis=1, keepdims=True)
@@ -96,7 +96,7 @@
             x[i] = ((v - average) * lax.rsqrt(spread + 1e-5) * gain_in).astype(BF16)
 
     def project(u, h):
-        @pl.loop(0, rows)
+        @pl.loop(0, rows, unroll=6)
         def _(i):
             w = weight_ref[i]
             p_t = lax.dot_general(wfull[h, u, : 4 * half], x[i], NT, preferred_element_type=F32)
@@ -155,7 +155,7 @@
         w_gate = gate_ref[u]
 
         def open_gates(first, count):
-            @pl.loop(0, count)
+            @pl.loop(0, count, unroll=6)
             def _(j):
                 gates[first + j] = jax.nn.sigmoid(
                     jnp.dot(x[first + j], w_gate, preferred_element_type=F32)
@@ -258,11 +258,11 @@
             return total, squares
 
         zero = jnp.zeros((rows, cols), F32)
-        total, squares = lax.fori_loop(0, slots, add, (zero, zero))
+        total, squares = lax.fori_loop(0, slots, add, (zero, zero), unroll=2)
         average = total / chans
         scale = lax.rsqrt(jnp.maximum(squares / chans - average * average, 0.0) + 1e-5)
 
-        @pl.loop(0, slots)
+        @pl.loop(0, slots, unroll=2)
         def _(q):
             for c in range(own):
                 at = pl.multiple_of((q * own + c) * rows_pad, 8)
@@ -277,7 +277,7 @@
             [wfull[h, u, 5 * half : 6 * half] for h in range(cores)], axis=0
         ).astype(F32)
 
-        @pl.loop(0, rows)
+        @pl.loop(0, rows, unroll=6)
         def _(i):
             scaled = jnp.concatenate(
                 [

time: 190 us -> 170 us (0.89)
  Pallas kernels: 182 us -> 162 us
    pallas_call x1, Pallas kernels: 182 us -> 162 us  [shards(): pl.pallas_call(functools.partial(kernel, dims), out_shape=jax.ShapeDtypeS...]
where the time goes in v4:
time: 170 us
  Pallas kernels  162 us (95%)
  local copies, waits for them, and re-layouts  4.74 us (3%)
  other arithmetic  2.35 us (1%)
    pallas_call x1, Pallas kernels, shards(): pl.pallas_call(functools.partial(kernel, dims), out_shape=jax.ShapeDtypeS...  162 us

profile of v4, /device:TPU:0, one launch (start us, length us, event | category | flops | bytes accessed | tf_op | source)
XLA Modules:
  0.0 169.7 jit_solution(18241760972322910313)
XLA Ops:
  0.7 0.1 dynamic_slice.7
  0.7 0.7 broadcast_in_dim.5
  1.5 0.8 multiply_multiply_fusion
  2.3 0.6 broadcast_in_dim.4.weight_ref
  2.9 1.5 pad_maximum_fusion.pack_ref
  4.5 162.0 %triangle.1 = bf16[24,384,128]{2,1,0:T(8,128)(2,1)} custom-call(bf16[48,384,128]{2,1,0:T(8,128)(2,1)} %pair_ref.1, f32[24,1,384]{2,1,0:T(1,128)} %broadcast_in_dim.4.weight_ref, bf16[2,192,128]{2,1,0:T(8,128)(2,1)} %pad_maximum_fusion.pack_ref, bf16[2,128]{1,0:T(2,128)(2,1)} %gain_ref.1, bf16[2,128,128]{2,1,0:T(8,128)(2,1)} %gate_ref.1), custom_call_target="tpu_custom_call" | custom-call | tf_op jit(solution)/shard_map/triangle/pallas_call | solution.py:341
  166.4 3.3 %copy.11 = bf16[24,384,128]{2,1,0:T(8,128)(2,1)} copy(bf16[24,384,128]{2,1,0:T(8,128)(2,1)} %triangle.1) | data formatting | bytes 4718592
  (1 shorter events, 0.0 us)

commit v5 on v4

--- a/solution.py
+++ b/solution.py
@@ -87,7 +87,7 @@
     def normalize_rows(u):
         gain_in = gain_ref[pl.ds(u, 1), :].astype(F32)
 
-        @pl.loop(0, rows, unroll=6)
+        @pl.loop(0, rows, unroll=(12 if rows % 12 == 0 else 6))
         def _(i):
             v = z[i].astype(F32)
             average = jnp.mean(v, axis=1, keepdims=True)
@@ -96,7 +96,7 @@
             x[i] = ((v - average) * lax.rsqrt(spread + 1e-5) * gain_in).astype(BF16)
 
     def project(u, h):
-        @pl.loop(0, rows, unroll=6)
+        @pl.loop(0, rows, unroll=(12 if rows % 12 == 0 else 6))
         def _(i):
             w = weight_ref[i]
             p_t = lax.dot_general(wfull[h, u, : 4 * half], x[i], NT, preferred_element_type=F32)
@@ -127,7 +127,7 @@
             h = (slot // slots_core + 1 + turn) % cores
             project(u, h)
 
-            @pl.loop(0, slots_core)
+            @pl.loop(0, slots_core, unroll=2)
             def _(s):
                 r = (slot + s) % slots_core
                 q = h * slots_core + r
@@ -153,9 +153,10 @@
 
         from_lr[slot] = to_lr[slot]
         w_gate = gate_ref[u]
+        zero = jnp.zeros((rows, cols), F32)
 
         def open_gates(first, count):
-            @pl.loop(0, count, unroll=6)
+            @pl.loop(0, count, unroll=(12 if rows % 12 == 0 else 6))
             def _(j):
                 gates[first + j] = jax.nn.sigmoid(
                     jnp.dot(x[first + j], w_gate, preferred_element_type=F32)
@@ -173,7 +174,7 @@
             def _(q):
                 arrival(1, to_lr.at[q, 1], recv_far, True, q).wait_recv()
 
-            @pl.loop(0, own)
+            @pl.loop(0, own, unroll=2)
             def _(c):
                 for q in range(slots):
                     at = pl.ds(q * rows, rows)
@@ -199,6 +200,15 @@
                 q = (slot + s) % slots
                 arrival(2, send_p.at[q], recv_p, False, q).wait_recv()
 
+            def add(q, sums):
+                total, squares = sums
+                for c in range(own):
+                    v = recv_p[q, c].astype(F32)
+                    total, squares = total + v, squares + v * v
+                return total, squares
+
+            total, squares = lax.fori_loop(0, slots, add, (zero, zero), unroll=2)
+
         else:
 
             @pl.loop(0, parts)
@@ -208,7 +218,7 @@
                     q = (slot + s) % slots
                     part_copy(0, to_lr.at[q], from_lr, False, q, g, q).wait_recv()
 
-                @pl.loop(0, part)
+                @pl.loop(0, part, unroll=2)
                 def _(d):
                     c = g * part + d
                     for q in range(slots):
@@ -235,30 +245,27 @@
             recv_q[0, slot] = send_q[side, slot]
             open_gates(0, rows)
 
-            @pl.loop(0, parts)
-            def _(g):
-                @pl.loop(0, slots)
-                def _(q):
-                    @pl.when(q != slot)
-                    def _():
-                        part_copy(1, send_q.at[side, q], recv_q.at[0], False, q, g, q).wait_recv()
-
-                    part_copy(2, send_q.at[1 - side, q], recv_q.at[1], True, q, g, q).wait_recv()
-                    for d in range(part):
-                        c = g * part + d
-                        recv_p[q, c] = (
-                            recv_q[0, q, c].astype(F32) + recv_q[1, q, c].astype(F32)
-                        ).astype(BF16)
-
-        def add(q, sums):
-            total, squares = sums
-            for c in range(own):
-                v = recv_p[q, c].astype(F32)
-                total, squares = total + v, squares + v * v
-            return total, squares
-
-        zero = jnp.zeros((rows, cols), F32)
-        total, squares = lax.fori_loop(0, slots, add, (zero, zero), unroll=2)
+            def take(step, sums):
+                g, q = step // slots, step % slots
+
+                @pl.when(q != slot)
+                def _():
+                    part_copy(1, send_q.at[side, q], recv_q.at[0], False, q, g, q).wait_recv()
+
+                part_copy(2, send_q.at[1 - side, q], recv_q.at[1], True, q, g, q).wait_recv()
+                total, squares = sums
+                for d in range(part):
+                    c = g * part + d
+                    value = (
+                        recv_q[0, q, c].astype(F32) + recv_q[1, q, c].astype(F32)
+                    ).astype(BF16)
+                    recv_p[q, c] = value
+                    v = value.astype(F32)
+                    total, squares = total + v, squares + v * v
+                return total, squares
+
+            total, squares = lax.fori_loop(0, parts * slots, take, (zero, zero))
+
         average = total / chans
         scale = lax.rsqrt(jnp.maximum(squares / chans - average * average, 0.0) + 1e-5)
 
@@ -277,7 +284,7 @@
             [wfull[h, u, 5 * half : 6 * half] for h in range(cores)], axis=0
         ).astype(F32)
 
-        @pl.loop(0, rows, unroll=6)
+        @pl.loop(0, rows, unroll=(12 if rows % 12 == 0 else 6))
         def _(i):
             scaled = jnp.concatenate(
                 [

time: 170 us -> 167 us (0.982)
  Pallas kernels: 162 us -> 159 us
    pallas_call x1, Pallas kernels: 162 us -> 159 us  [shards(): pl.pallas_call(functools.partial(kernel, dims), out_shape=jax.ShapeDtypeS...]
where the time goes in v5:
time: 167 us
  Pallas kernels  159 us (95%)
  local copies, waits for them, and re-layouts  4.74 us (3%)
  other arithmetic  2.35 us (1%)
    pallas_call x1, Pallas kernels, shards(): pl.pallas_call(functools.partial(kernel, dims), out_shape=jax.ShapeDtypeS...  159 us

profile of v5, /device:TPU:0, one launch (start us, length us, event | category | flops | bytes accessed | tf_op | source)
XLA Modules:
  0.0 166.9 jit_solution(12362894503437265417)
XLA Ops:
  0.7 0.1 dynamic_slice.7
  0.7 0.7 broadcast_in_dim.5
  1.5 0.8 multiply_multiply_fusion
  2.3 0.6 broadcast_in_dim.4.weight_ref
  2.9 1.5 pad_maximum_fusion.pack_ref
  4.5 159.2 %triangle.1 = bf16[24,384,128]{2,1,0:T(8,128)(2,1)} custom-call(bf16[48,384,128]{2,1,0:T(8,128)(2,1)} %pair_ref.1, f32[24,1,384]{2,1,0:T(1,128)} %broadcast_in_dim.4.weight_ref, bf16[2,192,128]{2,1,0:T(8,128)(2,1)} %pad_maximum_fusion.pack_ref, bf16[2,128]{1,0:T(2,128)(2,1)} %gain_ref.1, bf16[2,128,128]{2,1,0:T(8,128)(2,1)} %gate_ref.1), custom_call_target="tpu_custom_call" | custom-call | tf_op jit(solution)/shard_map/triangle/pallas_call | solution.py:348
  163.6 3.3 %copy.11 = bf16[24,384,128]{2,1,0:T(8,128)(2,1)} copy(bf16[24,384,128]{2,1,0:T(8,128)(2,1)} %triangle.1) | data formatting | bytes 4718592
  (1 shorter events, 0.0 us)
